TPU v7x, 32 devices: a whole 2x2x4 slice. The times are simulated.
32 devices in a mesh: space: 8 (over z, core), vel: 4 (over y, x).
Axes of the slice: x: 2, y: 2, z: 4, core: 2. Of those that a mesh axis runs over, the one named last changes fastest.
Arguments:
- distribution: float32 [64, 4, 4, 2, 16384], P('space', None, None, None, 'vel'), may hold values from 0 to 15, as said below
Outputs:
- evolved: float32 [64, 4, 4, 2, 16384], P('space', None, None, None, 'vel')
Inputs may be any that keep to these rules, and one draw needn't show every extreme that they name: `distribution`: every entry is non-negative.
All inputs are finite; a program needn't handle non-finite values.
Results may differ from a plain program's by a relative error of at most 0.0001.
Values sent between devices are 32-bit elements; how exact they have to be, the bound alone decides.
A program may use at most 64 MiB of HBM per device.

v0:
```python
import functools
import math

import jax
import jax.numpy as jnp
import ml_dtypes
import numpy as np
from jax import lax
from jax.experimental import pallas as pl
from jax.experimental.pallas import tpu as pltpu
from jax.sharding import PartitionSpec as P

NV = 32
STEPS = 3
SUB = 8
LANES = 128

speed_limit = 8.0
courant = 1.9
diffusivity_ratio = 2.0 / 3.0
encounter_rate = 0.7

SPACING = 2.0 * speed_limit / NV
QUADRATURE = SPACING**3 / (2.0 * math.pi) ** 1.5
COURANT_RATIO = courant / ((NV - 1) * speed_limit / NV)
PER_LANES = LANES // NV
MESH = pl.DeviceIdType.MESH
BLOCKS = [(0, 0), (0, 1), (0, 2), (0, 3), (1, 0), (1, 1), (1, 2), (2, 0), (2, 1), (3, 0)]
ROWS = 16


def moment_table():
    lane = np.arange(LANES)
    y = SPACING * (lane // NV - 0.5 * (PER_LANES - 1))
    z = -speed_limit + (lane % NV + 0.5) * SPACING
    one = np.ones(LANES)
    terms = {
        (0, 0): {0: one, 2: y, 3: z, 5: y * y, 6: z * z, 9: y * z, 11: y**3 + y * z * z, 12: z * y * y + z**3},
        (0, 1): {2: one, 5: 2 * y, 9: z, 11: 3 * y * y + z * z, 12: 2 * y * z},
        (0, 2): {5: one, 11: 3 * y, 12: z},
        (0, 3): {11: one},
        (1, 0): {1: one, 7: y, 8: z, 10: y * y + z * z},
        (1, 1): {7: one, 10: 2 * y},
        (1, 2): {10: one},
        (2, 0): {4: one, 11: y, 12: z},
        (2, 1): {11: one},
        (3, 0): {10: one},
    }
    table = np.zeros((len(BLOCKS) * LANES, ROWS))
    for place, block in enumerate(BLOCKS):
        for row, values in terms[block].items():
            table[place * LANES : (place + 1) * LANES, row] = values
    out = np.zeros((len(BLOCKS) * LANES, LANES), ml_dtypes.bfloat16)
    rest = table
    for part in range(3):
        piece = rest.astype(ml_dtypes.bfloat16)
        out[:, part * ROWS : (part + 1) * ROWS] = piece
        rest = rest - piece.astype(np.float64)
    return out


def field_rows(m, xi):
    rho = m[0]
    ux, uy, uz = m[1] / rho, m[2] / rho, m[3] / rho
    work = m[4] + m[5] + m[6]
    norm = ux * ux + uy * uy + uz * uz
    temp = (work / rho - norm) / 3.0
    along = ux * m[1] + uy * m[2] + uz * m[3]

    def heat(third, first, stress, u):
        return 0.5 * (
            third
            - 2.0 * (ux * stress[0] + uy * stress[1] + uz * stress[2])
            - u * work
            + norm * first
            + 2.0 * u * along
            - u * norm * rho
        )

    xheat = heat(m[10], m[1], (m[4], m[7], m[8]), ux)
    yheat = heat(m[11], m[2], (m[7], m[5], m[9]), uy)
    zheat = heat(m[12], m[3], (m[8], m[9], m[6]), uz)
    pressure = rho * temp
    conduct = (1.0 - diffusivity_ratio) / (5.0 * pressure * temp)
    root = jnp.sqrt(temp)
    amp = rho / (temp * root)
    retain = jnp.exp(-encounter_rate * rho * jnp.sqrt(root))
    inv = 1.0 / temp
    drift = xi - ux
    energy = drift * drift * inv
    height = (amp * (1.0 - retain)) * jnp.exp(-0.5 * energy)
    return height, energy - 5.0, drift * (conduct * xheat), [
        uy, uz, inv, conduct * yheat, conduct * zheat, retain,
    ]


def kernel(
    layers, cells, levels, spaces, vels,
    x_ref, w_ref, o_ref,
    stage, g_ref, r_ref, halo, sums, lhs, part, gathered, wide, table, table_halo,
    in_sem, out_sem, halo_send, halo_recv, tab_send, tab_recv, red_send, red_recv,
):
    f32 = jnp.float32
    s = lax.axis_index("space")
    v = lax.axis_index("vel")
    has_up = s < spaces - 1
    has_down = s > 0
    every = layers * cells
    nx = 2 * levels

    edge = 2
    spans = [(0, edge), (layers - edge, edge), (edge, layers - 2 * edge)]
    loads = []
    for i, (first, count) in enumerate(spans):
        rows = pl.ds(first * cells, count * cells)
        copy = pltpu.make_async_copy(x_ref.at[rows], stage.at[rows], in_sem.at[i])
        copy.start()
        loads.append(copy)

    barrier = pltpu.get_barrier_semaphore()
    for off in range(1, vels):
        pl.semaphore_signal(barrier, inc=1, device_id={"vel": lax.rem(v + off, vels)}, device_id_type=MESH)

    @pl.when(has_up)
    def _():
        pl.semaphore_signal(barrier, inc=1, device_id={"space": s + 1}, device_id_type=MESH)

    @pl.when(has_down)
    def _():
        pl.semaphore_signal(barrier, inc=1, device_id={"space": s - 1}, device_id_type=MESH)

    sub = lax.broadcasted_iota(jnp.int32, (SUB, LANES), 0)
    lane = lax.broadcasted_iota(jnp.int32, (SUB, LANES), 1)
    yv = -speed_limit + ((sub * PER_LANES + lane // NV).astype(f32) + 0.5) * SPACING
    zv = -speed_limit + ((lane % NV).astype(f32) + 0.5) * SPACING
    first_level = v * levels

    def speed(a):
        return ((first_level + a).astype(f32) + 0.5) * SPACING

    place = lax.broadcasted_iota(jnp.int32, (nx, every), 0)
    ahead = place >= levels
    level = jnp.where(ahead, place - levels, place) + first_level
    xi = jnp.where(ahead, 1.0, -1.0) * ((level.astype(f32) + 0.5) * SPACING)

    def sweep_coefs(speeds):
        n = COURANT_RATIO * jnp.abs(speeds)
        near = n * (2.0 - n)
        return near, 1.0 - n, jnp.where(speeds > 0.0, -near, near)

    ycoefs = sweep_coefs(yv)
    zcoefs = sweep_coefs(zv)

    def unpack(half, first, count):
        def body(i, _):
            for a in range(levels):
                g_ref[0, half, a, first + i // cells, i % cells] = stage[
                    first * cells + i, pl.ds(a * 2 * SUB + half, SUB, stride=2), :
                ]
            return 0

        lax.fori_loop(0, count * cells, body, 0, unroll=4)

    def stage_one(which, first, count):
        squares = []
        speeds = []
        for a in range(levels):
            xa = speed(jnp.int32(a))
            speeds.append(xa)
            squares.append(xa * xa)

        def body(i, _):
            layer = first + i // cells
            cell = i % cells
            total = [None] * 4
            for a in range(levels):
                back = g_ref[which, 0, a, layer, cell]
                fore = g_ref[which, 1, a, layer, cell]
                even = fore + back
                odd = (fore - back) * speeds[a]
                terms = [even, odd, even * squares[a], odd * squares[a]]
                total = [t if o is None else o + t for o, t in zip(total, terms)]
            at = (layer * cells + cell) * SUB
            for m in range(4):
                sums[m, pl.ds(at, SUB), :] = total[m]
            return 0

        lax.fori_loop(0, count * cells, body, 0, unroll=4)

    def stage_two():
        heights = [2.0 * SPACING * (PER_LANES / 4) * (2 * j - (SUB - 1)) for j in range(SUB)]

        def body(i, _):
            at = pl.multiple_of(i * SUB, SUB)
            for m, powers in enumerate((4, 3, 2, 1)):
                rows = [sums[m, pl.ds(at * SUB + j, SUB, stride=SUB), :] for j in range(SUB)]
                total = [None] * powers
                for j in range(SUB // 2):
                    low, high = rows[j], rows[SUB - 1 - j]
                    size = heights[SUB - 1 - j]
                    even = high + low
                    odd = (high - low) * size if powers > 1 else None
                    terms = [even, odd]
                    if powers > 2:
                        terms.append(even * (size * size))
                    if powers > 3:
                        terms.append(odd * (size * size))
                    total = [t if o is None else o + t for o, t in zip(total, terms[:powers])]
                for p in range(powers):
                    q = BLOCKS.index((m, p))
                    lhs[pl.ds(at, SUB), q * LANES : (q + 1) * LANES] = total[p]
            return 0

        lax.fori_loop(0, every // SUB, body, 0, unroll=2)

    def reduce_copy(k, off):
        return pltpu.make_async_remote_copy(
            src_ref=part.at[k],
            dst_ref=gathered.at[k, off - 1],
            send_sem=red_send.at[k, off - 1],
            recv_sem=red_recv.at[k, off - 1],
            device_id={"vel": lax.rem(v + off, vels)},
            device_id_type=MESH,
        )

    def table_copy(k, half):
        first = (layers - edge) * cells if half else 0
        return pltpu.make_async_remote_copy(
            src_ref=table.at[k, pl.ds(first, edge * cells)],
            dst_ref=table_halo.at[k, half],
            send_sem=tab_send.at[k, half],
            recv_sem=tab_recv.at[k, half],
            device_id={"space": s + 1 if half else s - 1},
            device_id_type=MESH,
        )

    def halo_copy(k, half):
        first = layers - edge if half else 0
        return pltpu.make_async_remote_copy(
            src_ref=g_ref.at[k % 2, half, :, pl.ds(first, edge)],
            dst_ref=halo.at[k, half],
            send_sem=halo_send.at[k, half],
            recv_sem=halo_recv.at[k, half],
            device_id={"space": s + 1 if half else s - 1},
            device_id_type=MESH,
        )

    sends = {0: has_down, 1: has_up}
    receives = {0: has_up, 1: has_down}

    def fields(k):
        stage_two()
        rest = lhs[...]
        acc = None
        for _ in range(3):
            piece = rest.astype(jnp.bfloat16)
            term = jnp.dot(piece, w_ref[...], preferred_element_type=f32)
            acc = term if acc is None else acc + term
            rest = rest - piece.astype(f32)
        turned = acc.T
        part[k] = (turned[0:ROWS] + turned[ROWS : 2 * ROWS] + turned[2 * ROWS : 3 * ROWS]) * QUADRATURE
        for off in range(1, vels):
            reduce_copy(k, off).start()
        total = part[k]
        for off in range(1, vels):
            reduce_copy(k, off).wait_recv()
            total = total + gathered[k, off - 1]
        m = [total[i : i + 1, :] for i in range(13)]
        height, energy, heat, rest = field_rows(m, xi)
        wide[0:nx, :] = height
        wide[nx : 2 * nx, :] = energy
        wide[2 * nx : 3 * nx, :] = heat
        for i, row in enumerate(rest):
            wide[3 * nx + i : 3 * nx + i + 1, :] = row
        table[k] = wide[...].T
        for half in range(2):
            @pl.when(sends[half])
            def _():
                table_copy(k, half).start()

    def relax_cell(row, halves, load, store):
        def spread(i):
            return jnp.broadcast_to(row[:, i : i + 1], (SUB, LANES))

        uy, uz, inv, qy, qz, retain = [spread(3 * nx + i) for i in range(6)]
        cy = yv - uy
        cz = zv - uz
        energy = (cy * cy + cz * cz) * inv
        heat = cy * qy + cz * qz
        gauss = jnp.exp(-0.5 * energy)
        for half in halves:
            for a in range(levels):
                i = half * levels + a
                bracket = 1.0 + (spread(2 * nx + i) + heat) * (spread(nx + i) + energy)
                store(half, a, (spread(i) * gauss) * bracket + load(half, a) * retain)

    def relax_own(k):
        def body(i, _):
            layer = i // cells
            cell = i % cells

            def load(half, a):
                return g_ref[k % 2, half, a, layer, cell]

            def store(half, a, value):
                r_ref[half, a, layer + edge * half, cell] = value

            relax_cell(table[k, pl.ds(i, 1), :], (0, 1), load, store)
            return 0

        lax.fori_loop(0, every, body, 0, unroll=2)

    def relax_halo(k, half):
        def body(i, _):
            layer = i // cells
            cell = i % cells

            def load(half, a):
                return halo[k, half, a, layer, cell]

            def store(half, a, value):
                r_ref[half, a, layer + (0 if half else layers), cell] = value

            relax_cell(table_halo[k, half, pl.ds(i, 1), :], (half,), load, store)
            return 0

        lax.fori_loop(0, edge * cells, body, 0, unroll=2)

    def periodic(values, coefs):
        near, keep, turn = coefs
        even, odd = values[0] + values[2], values[1] + values[3]
        deven, dodd = values[0] - values[2], values[1] - values[3]
        shift = near * (odd - even)
        e, o = even + shift, odd - shift
        de = keep * deven + turn * dodd
        do = keep * dodd - turn * deven
        return [e + de, o + do, e - de, o - do]

    def transport(k, half, first, count):
        last = k == STEPS - 1

        def body(i, _):
            a = i // count
            layer = first + i % count
            n = COURANT_RATIO * speed(a)
            own = 0.25 * (1.0 - n) * (1.0 - 0.5 * n)
            near = 0.25 * n * (2.0 - n)
            far = 0.125 * n * (n - 1.0)
            back = (2, 1, 0) if half else (0, 1, 2)
            moved = []
            for c in range(cells):
                r0, r1, r2 = [r_ref[half, a, layer + b, c] for b in back]
                moved.append(own * r0 + near * r1 + far * r2)
            for z in range(4):
                moved[z::4] = periodic(moved[z::4], ycoefs)
            for y in range(4):
                moved[4 * y : 4 * y + 4] = periodic(moved[4 * y : 4 * y + 4], zcoefs)
            for c in range(cells):
                if last:
                    stage[layer * cells + c, pl.ds(a * 2 * SUB + half, SUB, stride=2), :] = moved[c]
                else:
                    g_ref[(k + 1) % 2, half, a, layer, c] = moved[c]
            return 0

        lax.fori_loop(0, levels * count, body, 0, unroll=2)

    for half in range(2):
        @pl.when(jnp.logical_not(receives[half]))
        def _():
            for a in range(levels):
                for layer in range(edge):
                    r_ref[half, a, layer + (0 if half else layers)] = jnp.zeros((cells, SUB, LANES), f32)

    wide[...] = jnp.zeros_like(wide)

    loads[0].wait()
    unpack(0, 0, edge)
    loads[1].wait()
    unpack(1, layers - edge, edge)

    greeted = vels - 1 + jnp.minimum(s, 1) + jnp.minimum(spaces - 1 - s, 1)
    pl.semaphore_wait(barrier, greeted)

    for half in range(2):
        @pl.when(sends[half])
        def _():
            halo_copy(0, half).start()

    unpack(1, 0, edge)
    unpack(0, layers - edge, edge)
    stage_one(0, 0, edge)
    stage_one(0, layers - edge, edge)
    loads[2].wait()
    unpack(0, edge, layers - 2 * edge)
    unpack(1, edge, layers - 2 * edge)
    stage_one(0, edge, layers - 2 * edge)

    stores = []

    def store_out(i):
        first, count = spans[i]
        rows = pl.ds(first * cells, count * cells)
        copy = pltpu.make_async_copy(stage.at[rows], o_ref.at[rows], out_sem.at[i])
        copy.start()
        stores.append(copy)

    for k in range(STEPS):
        last = k == STEPS - 1
        fields(k)
        relax_own(k)
        transport(k, 1, layers - edge, edge)
        transport(k, 0, 0, edge)
        if not last:
            for half in range(2):
                @pl.when(sends[half])
                def _():
                    halo_copy(k + 1, half).start()
        for half in range(2):
            transport(k, half, edge, layers - 2 * edge)
        if last:
            store_out(2)
        else:
            stage_one((k + 1) % 2, edge, layers - 2 * edge)
        for half in range(2):
            @pl.when(receives[half])
            def _():
                table_copy(k, half).wait_recv()
                halo_copy(k, half).wait_recv()
                relax_halo(k, half)

            transport(k, half, 0 if half else layers - edge, edge)
            span = 0 if half else 1
            if last:
                store_out(span)
            else:
                stage_one((k + 1) % 2, spans[span][0], edge)
        for half in range(2):
            @pl.when(sends[half])
            def _():
                table_copy(k, half).wait_send()
                halo_copy(k, half).wait_send()
        for off in range(1, vels):
            reduce_copy(k, off).wait_send()

    for copy in stores:
        copy.wait()


def local(distribution, weights, spaces, vels):
    layers, breadth, height, halves, velocities = distribution.shape
    cells = breadth * height
    assert breadth == 4 and height == 4 and halves == 2
    levels = velocities // (NV * NV)
    tiles = velocities // LANES
    every = layers * cells
    rows = distribution.reshape(every, halves, tiles, LANES)
    rows = rows.transpose(0, 2, 1, 3).reshape(every, tiles * halves, LANES)
    f32 = jnp.float32
    dma = pltpu.SemaphoreType.DMA
    out = pl.pallas_call(
        functools.partial(kernel, layers, cells, levels, spaces, vels),
        out_shape=jax.ShapeDtypeStruct(rows.shape, f32),
        in_specs=[
            pl.BlockSpec(memory_space=pl.ANY),
            pl.BlockSpec(memory_space=pltpu.VMEM),
        ],
        out_specs=pl.BlockSpec(memory_space=pl.ANY),
        scratch_shapes=[
            pltpu.VMEM(rows.shape, f32),
            pltpu.VMEM((2, 2, levels, layers, cells, SUB, LANES), f32),
            pltpu.VMEM((2, levels, layers + 2, cells, SUB, LANES), f32),
            pltpu.VMEM((STEPS, 2, levels, 2, cells, SUB, LANES), f32),
            pltpu.VMEM((4, every * SUB, LANES), f32),
            pltpu.VMEM((every, len(BLOCKS) * LANES), f32),
            pltpu.VMEM((STEPS, ROWS, every), f32),
            pltpu.VMEM((STEPS, max(vels - 1, 1), ROWS, every), f32),
            pltpu.VMEM((LANES, every), f32),
            pltpu.VMEM((STEPS, every, LANES), f32),
            pltpu.VMEM((STEPS, 2, 2 * cells, LANES), f32),
            dma((3,)),
            dma((3,)),
            dma((STEPS, 2)),
            dma((STEPS, 2)),
            dma((STEPS, 2)),
            dma((STEPS, 2)),
            dma((STEPS, max(vels - 1, 1))),
            dma((STEPS, max(vels - 1, 1))),
        ],
        compiler_params=pltpu.CompilerParams(
            collective_id=0, has_side_effects=True, vmem_limit_bytes=48 * 2**20
        ),
    )(rows, weights)
    out = out.reshape(every, tiles, halves, LANES).transpose(0, 2, 1, 3)
    return out.reshape(distribution.shape)


def solution(mesh):
    weights = moment_table()
    spec = P("space", None, None, None, "vel")
    body = functools.partial(local, spaces=mesh.shape["space"], vels=mesh.shape["vel"])
    mapped = jax.shard_map(
        body, mesh=mesh, in_specs=(spec, P()), out_specs=spec, check_vma=False
    )
    return lambda distribution: mapped(distribution, jnp.asarray(weights))
```

profile of v0, /device:TPU:8, one launch (start us, length us, event | category | flops | bytes accessed | tf_op | source)
XLA Modules:
  0.0 80.9 jit_solution(16332808416607912106)
XLA Ops:
  0.0 0.0 copy-start
  0.0 1.0 %copy-done = bf16[1280,128]{1,0:T(8,128)(2,1)S(1)} copy-done((bf16[1280,128]{1,0:T(8,128)(2,1)S(1)}, bf16[1280,128]{1,0:T(8,128)(2,1)}, u32[]{:S(2)}) %copy-start) | copy-done | bytes 327704
  1.0 77.9 %shard_map.28 = f32[128,64,128]{2,1,0:T(8,128)S(1)} custom-call(f32[128,64,128]{2,1,0:T(8,128)} %bitcast.11, bf16[1280,128]{1,0:T(8,128)(2,1)S(1)} %copy-done), custom_call_target="tpu_custom_call" | custom-call | tf_op jit(solution)/shard_map/pallas_call | solution.py:460
  78.9 2.0 %copy.6 = f32[8,4,4,2,4096]{4,3,2,1,0:T(2,128)} copy(f32[8,4,4,2,4096]{4,3,2,1,0:T(2,128)S(1)} %bitcast.10) | data formatting | bytes 8388608
Async XLA Ops:
  0.0 1.0 %copy-start = (bf16[1280,128]{1,0:T(8,128)(2,1)S(1)}, bf16[1280,128]{1,0:T(8,128)(2,1)}, u32[]{:S(2)}) copy-start(bf16[1280,128]{1,0:T(8,128)(2,1)} %constant.2.clone.w_ref) | copy-start | bytes 983044
where the time goes:
time: 81 us; the launch traced here: 80.9 us
  Pallas kernels  77.9 us (96%)
  local copies, waits for them, and re-layouts  2.99 us (4%)
    pallas_call x1, Pallas kernels, local(): pl.pallas_call(functools.partial(kernel, layers, cells, levels, spaces, v...  77.9 us
    unnamed x3, local copies, waits for them, and re-layouts  2.99 us

commit v1 on v0

--- a/solution.py
+++ b/solution.py
@@ -97,7 +97,8 @@
 def kernel(
     layers, cells, levels, spaces, vels,
     x_ref, w_ref, o_ref,
-    stage, g_ref, r_ref, halo, sums, lhs, part, gathered, wide, table, table_halo,
+    stage, g_ref, r_ref, halo, sums, lhs, part, gathered, tall, wide, table, table_halo,
+    splat, splat_halo,
     in_sem, out_sem, halo_send, halo_recv, tab_send, tab_recv, red_send, red_recv,
 ):
     f32 = jnp.float32
@@ -110,6 +111,9 @@
 
     edge = 2
     spans = [(0, edge), (layers - edge, edge), (edge, layers - 2 * edge)]
+    groups = [spans[:2], spans[2:]]
+    starts = [0, 2 * edge * cells]
+    sizes = [sum(n for _, n in group) * cells for group in groups]
     loads = []
     for i, (first, count) in enumerate(spans):
         rows = pl.ds(first * cells, count * cells)
@@ -138,7 +142,7 @@
     def speed(a):
         return ((first_level + a).astype(f32) + 0.5) * SPACING
 
-    place = lax.broadcasted_iota(jnp.int32, (nx, every), 0)
+    place = lax.broadcasted_iota(jnp.int32, (nx, LANES), 0)
     ahead = place >= levels
     level = jnp.where(ahead, place - levels, place) + first_level
     xi = jnp.where(ahead, 1.0, -1.0) * ((level.astype(f32) + 0.5) * SPACING)
@@ -187,11 +191,12 @@
 
         lax.fori_loop(0, count * cells, body, 0, unroll=4)
 
-    def stage_two():
+    def stage_two(first, count, row):
         heights = [2.0 * SPACING * (PER_LANES / 4) * (2 * j - (SUB - 1)) for j in range(SUB)]
 
         def body(i, _):
-            at = pl.multiple_of(i * SUB, SUB)
+            at = first * cells + i * SUB
+            to = pl.multiple_of(row + i * SUB, SUB)
             for m, powers in enumerate((4, 3, 2, 1)):
                 rows = [sums[m, pl.ds(at * SUB + j, SUB, stride=SUB), :] for j in range(SUB)]
                 total = [None] * powers
@@ -208,25 +213,25 @@
                     total = [t if o is None else o + t for o, t in zip(total, terms[:powers])]
                 for p in range(powers):
                     q = BLOCKS.index((m, p))
-                    lhs[pl.ds(at, SUB), q * LANES : (q + 1) * LANES] = total[p]
-            return 0
-
-        lax.fori_loop(0, every // SUB, body, 0, unroll=2)
-
-    def reduce_copy(k, off):
+                    lhs[pl.ds(to, SUB), q * LANES : (q + 1) * LANES] = total[p]
+            return 0
+
+        lax.fori_loop(0, count * cells // SUB, body, 0, unroll=2)
+
+    def reduce_copy(k, which, off):
         return pltpu.make_async_remote_copy(
-            src_ref=part.at[k],
-            dst_ref=gathered.at[k, off - 1],
-            send_sem=red_send.at[k, off - 1],
-            recv_sem=red_recv.at[k, off - 1],
+            src_ref=part.at[k, which],
+            dst_ref=gathered.at[k, which, off - 1],
+            send_sem=red_send.at[k, which, off - 1],
+            recv_sem=red_recv.at[k, which, off - 1],
             device_id={"vel": lax.rem(v + off, vels)},
             device_id_type=MESH,
         )
 
     def table_copy(k, half):
-        first = (layers - edge) * cells if half else 0
+        first = edge * cells if half else 0
         return pltpu.make_async_remote_copy(
-            src_ref=table.at[k, pl.ds(first, edge * cells)],
+            src_ref=table.at[k, 0, pl.ds(first, edge * cells)],
             dst_ref=table_halo.at[k, half],
             send_sem=tab_send.at[k, half],
             recv_sem=tab_recv.at[k, half],
@@ -248,23 +253,43 @@
     sends = {0: has_down, 1: has_up}
     receives = {0: has_up, 1: has_down}
 
-    def fields(k):
-        stage_two()
-        rest = lhs[...]
+    def moments(k, which):
+        row = starts[which]
+        for first, count in groups[which]:
+            stage_two(first, count, row)
+            row += count * cells
+        size = sizes[which]
+        rest = lhs[starts[which] : starts[which] + size, :]
         acc = None
         for _ in range(3):
             piece = rest.astype(jnp.bfloat16)
             term = jnp.dot(piece, w_ref[...], preferred_element_type=f32)
             acc = term if acc is None else acc + term
             rest = rest - piece.astype(f32)
-        turned = acc.T
-        part[k] = (turned[0:ROWS] + turned[ROWS : 2 * ROWS] + turned[2 * ROWS : 3 * ROWS]) * QUADRATURE
+        tall[0:size, :] = acc
+        turned = tall[...].T
+        part[k, which] = (
+            turned[0:ROWS] + turned[ROWS : 2 * ROWS] + turned[2 * ROWS : 3 * ROWS]
+        ) * QUADRATURE
         for off in range(1, vels):
-            reduce_copy(k, off).start()
-        total = part[k]
+            reduce_copy(k, which, off).start()
+
+    def fill(source, target, rows, start):
+        def body(i, _):
+            at = pl.multiple_of(i * SUB, SUB)
+            block = source[pl.ds(at, SUB), :]
+            to = pl.multiple_of(start + i * SUB, SUB)
+            for c in range(3 * nx + 6):
+                target[c, pl.ds(to, SUB), :] = jnp.broadcast_to(block[:, c : c + 1], (SUB, LANES))
+            return 0
+
+        lax.fori_loop(0, rows // SUB, body, 0)
+
+    def fields(k, which):
+        total = part[k, which]
         for off in range(1, vels):
-            reduce_copy(k, off).wait_recv()
-            total = total + gathered[k, off - 1]
+            reduce_copy(k, which, off).wait_recv()
+            total = total + gathered[k, which, off - 1]
         m = [total[i : i + 1, :] for i in range(13)]
         height, energy, heat, rest = field_rows(m, xi)
         wide[0:nx, :] = height
@@ -272,15 +297,17 @@
         wide[2 * nx : 3 * nx, :] = heat
         for i, row in enumerate(rest):
             wide[3 * nx + i : 3 * nx + i + 1, :] = row
-        table[k] = wide[...].T
-        for half in range(2):
-            @pl.when(sends[half])
-            def _():
-                table_copy(k, half).start()
-
-    def relax_cell(row, halves, load, store):
+        table[k, which] = wide[...].T
+        if which == 0:
+            for half in range(2):
+                @pl.when(sends[half])
+                def _():
+                    table_copy(k, half).start()
+        fill(table.at[k, which], splat, sizes[which], starts[which])
+
+    def relax_cell(source, row, halves, load, store):
         def spread(i):
-            return jnp.broadcast_to(row[:, i : i + 1], (SUB, LANES))
+            return source[i, pl.ds(row, 1), :]
 
         uy, uz, inv, qy, qz, retain = [spread(3 * nx + i) for i in range(6)]
         cy = yv - uy
@@ -294,36 +321,44 @@
                 bracket = 1.0 + (spread(2 * nx + i) + heat) * (spread(nx + i) + energy)
                 store(half, a, (spread(i) * gauss) * bracket + load(half, a) * retain)
 
-    def relax_own(k):
+    def relax_own(k, first, count, row):
+        def body(i, _):
+            layer = first + i // cells
+            cell = i % cells
+
+            def load(half, a):
+                return g_ref[k % 2, half, a, layer, cell]
+
+            def store(half, a, value):
+                r_ref[half, a, layer + edge * half, cell] = value
+
+            relax_cell(splat, row + i, (0, 1), load, store)
+            return 0
+
+        lax.fori_loop(0, count * cells, body, 0, unroll=2)
+
+    def relax_group(k, which):
+        fields(k, which)
+        row = starts[which]
+        for first, count in groups[which]:
+            relax_own(k, first, count, row)
+            row += count * cells
+
+    def relax_halo(k, half):
         def body(i, _):
             layer = i // cells
             cell = i % cells
 
             def load(half, a):
-                return g_ref[k % 2, half, a, layer, cell]
-
-            def store(half, a, value):
-                r_ref[half, a, layer + edge * half, cell] = value
-
-            relax_cell(table[k, pl.ds(i, 1), :], (0, 1), load, store)
-            return 0
-
-        lax.fori_loop(0, every, body, 0, unroll=2)
-
-    def relax_halo(k, half):
-        def body(i, _):
-            layer = i // cells
-            cell = i % cells
-
-            def load(half, a):
                 return halo[k, half, a, layer, cell]
 
             def store(half, a, value):
                 r_ref[half, a, layer + (0 if half else layers), cell] = value
 
-            relax_cell(table_halo[k, half, pl.ds(i, 1), :], (half,), load, store)
-            return 0
-
+            relax_cell(splat_halo, i, (half,), load, store)
+            return 0
+
+        fill(table_halo.at[k, half], splat_halo, edge * cells, 0)
         lax.fori_loop(0, edge * cells, body, 0, unroll=2)
 
     def periodic(values, coefs):
@@ -372,6 +407,7 @@
                     r_ref[half, a, layer + (0 if half else layers)] = jnp.zeros((cells, SUB, LANES), f32)
 
     wide[...] = jnp.zeros_like(wide)
+    tall[...] = jnp.zeros_like(tall)
 
     loads[0].wait()
     unpack(0, 0, edge)
@@ -390,10 +426,12 @@
     unpack(0, layers - edge, edge)
     stage_one(0, 0, edge)
     stage_one(0, layers - edge, edge)
+    moments(0, 0)
     loads[2].wait()
     unpack(0, edge, layers - 2 * edge)
     unpack(1, edge, layers - 2 * edge)
     stage_one(0, edge, layers - 2 * edge)
+    moments(0, 1)
 
     stores = []
 
@@ -406,8 +444,8 @@
 
     for k in range(STEPS):
         last = k == STEPS - 1
-        fields(k)
-        relax_own(k)
+        for which in (0, 1) if k == 0 else (1, 0):
+            relax_group(k, which)
         transport(k, 1, layers - edge, edge)
         transport(k, 0, 0, edge)
         if not last:
@@ -421,6 +459,7 @@
             store_out(2)
         else:
             stage_one((k + 1) % 2, edge, layers - 2 * edge)
+            moments(k + 1, 1)
         for half in range(2):
             @pl.when(receives[half])
             def _():
@@ -434,13 +473,16 @@
                 store_out(span)
             else:
                 stage_one((k + 1) % 2, spans[span][0], edge)
+        if not last:
+            moments(k + 1, 0)
         for half in range(2):
             @pl.when(sends[half])
             def _():
                 table_copy(k, half).wait_send()
                 halo_copy(k, half).wait_send()
-        for off in range(1, vels):
-            reduce_copy(k, off).wait_send()
+        for which in range(2):
+            for off in range(1, vels):
+                reduce_copy(k, which, off).wait_send()
 
     for copy in stores:
         copy.wait()
@@ -450,6 +492,7 @@
     layers, breadth, height, halves, velocities = distribution.shape
     cells = breadth * height
     assert breadth == 4 and height == 4 and halves == 2
+    assert layers > 4 and (layers - 4) * cells <= LANES
     levels = velocities // (NV * NV)
     tiles = velocities // LANES
     every = layers * cells
@@ -472,19 +515,22 @@
             pltpu.VMEM((STEPS, 2, levels, 2, cells, SUB, LANES), f32),
             pltpu.VMEM((4, every * SUB, LANES), f32),
             pltpu.VMEM((every, len(BLOCKS) * LANES), f32),
-            pltpu.VMEM((STEPS, ROWS, every), f32),
-            pltpu.VMEM((STEPS, max(vels - 1, 1), ROWS, every), f32),
-            pltpu.VMEM((LANES, every), f32),
-            pltpu.VMEM((STEPS, every, LANES), f32),
+            pltpu.VMEM((STEPS, 2, ROWS, LANES), f32),
+            pltpu.VMEM((STEPS, 2, max(vels - 1, 1), ROWS, LANES), f32),
+            pltpu.VMEM((LANES, LANES), f32),
+            pltpu.VMEM((LANES, LANES), f32),
+            pltpu.VMEM((STEPS, 2, LANES, LANES), f32),
             pltpu.VMEM((STEPS, 2, 2 * cells, LANES), f32),
+            pltpu.VMEM((6 * levels + 6, every, LANES), f32),
+            pltpu.VMEM((6 * levels + 6, 2 * cells, LANES), f32),
             dma((3,)),
             dma((3,)),
             dma((STEPS, 2)),
             dma((STEPS, 2)),
             dma((STEPS, 2)),
             dma((STEPS, 2)),
-            dma((STEPS, max(vels - 1, 1))),
-            dma((STEPS, max(vels - 1, 1))),
+            dma((STEPS, 2, max(vels - 1, 1))),
+            dma((STEPS, 2, max(vels - 1, 1))),
         ],
         compiler_params=pltpu.CompilerParams(
             collective_id=0, has_side_effects=True, vmem_limit_bytes=48 * 2**20

time: 81 us -> 45.2 us (0.56)
  Pallas kernels: 77.9 us -> 42.1 us
    pallas_call x1, Pallas kernels: 77.9 us -> 42.1 us  [local(): pl.pallas_call(functools.partial(kernel, layers, cells, levels, spaces, v...]
where the time goes in v1:
time: 45.2 us; the launch traced here: 45.1 us
  Pallas kernels  42.1 us (93%)
  local copies, waits for them, and re-layouts  2.99 us (7%)
    pallas_call x1, Pallas kernels, local(): pl.pallas_call(functools.partial(kernel, layers, cells, levels, spaces, v...  42.1 us
    unnamed x3, local copies, waits for them, and re-layouts  2.99 us

profile of v1, /device:TPU:8, one launch (start us, length us, event | category | flops | bytes accessed | tf_op | source)
XLA Modules:
  0.0 45.1 jit_solution(17950219795715355721)
XLA Ops:
  0.0 0.0 copy-start
  0.0 1.0 %copy-done = bf16[1280,128]{1,0:T(8,128)(2,1)S(1)} copy-done((bf16[1280,128]{1,0:T(8,128)(2,1)S(1)}, bf16[1280,128]{1,0:T(8,128)(2,1)}, u32[]{:S(2)}) %copy-start) | copy-done | bytes 327704
  1.0 42.1 %shard_map.28 = f32[128,64,128]{2,1,0:T(8,128)S(1)} custom-call(f32[128,64,128]{2,1,0:T(8,128)} %bitcast.11, bf16[1280,128]{1,0:T(8,128)(2,1)S(1)} %copy-done), custom_call_target="tpu_custom_call" | custom-call | tf_op jit(solution)/shard_map/pallas_call | solution.py:503
  43.0 2.0 %copy.6 = f32[8,4,4,2,4096]{4,3,2,1,0:T(2,128)} copy(f32[8,4,4,2,4096]{4,3,2,1,0:T(2,128)S(1)} %bitcast.10) | data formatting | bytes 8388608
Async XLA Ops:
  0.0 1.0 %copy-start = (bf16[1280,128]{1,0:T(8,128)(2,1)S(1)}, bf16[1280,128]{1,0:T(8,128)(2,1)}, u32[]{:S(2)}) copy-start(bf16[1280,128]{1,0:T(8,128)(2,1)} %constant.2.clone.w_ref) | copy-start | bytes 983044

commit v2 on v1

--- a/solution.py
+++ b/solution.py
@@ -99,7 +99,7 @@
     x_ref, w_ref, o_ref,
     stage, g_ref, r_ref, halo, sums, lhs, part, gathered, tall, wide, table, table_halo,
     splat, splat_halo,
-    in_sem, out_sem, halo_send, halo_recv, tab_send, tab_recv, red_send, red_recv,
+    in_sem, halo_send, halo_recv, tab_send, tab_recv, red_send, red_recv,
 ):
     f32 = jnp.float32
     s = lax.axis_index("space")
@@ -260,13 +260,12 @@
             row += count * cells
         size = sizes[which]
         rest = lhs[starts[which] : starts[which] + size, :]
-        acc = None
+        pieces = []
         for _ in range(3):
-            piece = rest.astype(jnp.bfloat16)
-            term = jnp.dot(piece, w_ref[...], preferred_element_type=f32)
-            acc = term if acc is None else acc + term
-            rest = rest - piece.astype(f32)
-        tall[0:size, :] = acc
+            pieces.append(rest.astype(jnp.bfloat16))
+            rest = rest - pieces[-1].astype(f32)
+        product = jnp.dot(jnp.concatenate(pieces, axis=0), w_ref[...], preferred_element_type=f32)
+        tall[0:size, :] = product[0:size] + product[size : 2 * size] + product[2 * size : 3 * size]
         turned = tall[...].T
         part[k, which] = (
             turned[0:ROWS] + turned[ROWS : 2 * ROWS] + turned[2 * ROWS : 3 * ROWS]
@@ -283,7 +282,7 @@
                 target[c, pl.ds(to, SUB), :] = jnp.broadcast_to(block[:, c : c + 1], (SUB, LANES))
             return 0
 
-        lax.fori_loop(0, rows // SUB, body, 0)
+        lax.fori_loop(0, rows // SUB, body, 0, unroll=4)
 
     def fields(k, which):
         total = part[k, which]
@@ -392,7 +391,7 @@
                 moved[4 * y : 4 * y + 4] = periodic(moved[4 * y : 4 * y + 4], zcoefs)
             for c in range(cells):
                 if last:
-                    stage[layer * cells + c, pl.ds(a * 2 * SUB + half, SUB, stride=2), :] = moved[c]
+                    o_ref[layer * cells + c, pl.ds(a * 2 * SUB + half, SUB, stride=2), :] = moved[c]
                 else:
                     g_ref[(k + 1) % 2, half, a, layer, c] = moved[c]
             return 0
@@ -432,15 +431,6 @@
     unpack(1, edge, layers - 2 * edge)
     stage_one(0, edge, layers - 2 * edge)
     moments(0, 1)
-
-    stores = []
-
-    def store_out(i):
-        first, count = spans[i]
-        rows = pl.ds(first * cells, count * cells)
-        copy = pltpu.make_async_copy(stage.at[rows], o_ref.at[rows], out_sem.at[i])
-        copy.start()
-        stores.append(copy)
 
     for k in range(STEPS):
         last = k == STEPS - 1
@@ -455,9 +445,7 @@
                     halo_copy(k + 1, half).start()
         for half in range(2):
             transport(k, half, edge, layers - 2 * edge)
-        if last:
-            store_out(2)
-        else:
+        if not last:
             stage_one((k + 1) % 2, edge, layers - 2 * edge)
             moments(k + 1, 1)
         for half in range(2):
@@ -469,9 +457,7 @@
 
             transport(k, half, 0 if half else layers - edge, edge)
             span = 0 if half else 1
-            if last:
-                store_out(span)
-            else:
+            if not last:
                 stage_one((k + 1) % 2, spans[span][0], edge)
         if not last:
             moments(k + 1, 0)
@@ -483,9 +469,6 @@
         for which in range(2):
             for off in range(1, vels):
                 reduce_copy(k, which, off).wait_send()
-
-    for copy in stores:
-        copy.wait()
 
 
 def local(distribution, weights, spaces, vels):
@@ -507,7 +490,7 @@
             pl.BlockSpec(memory_space=pl.ANY),
             pl.BlockSpec(memory_space=pltpu.VMEM),
         ],
-        out_specs=pl.BlockSpec(memory_space=pl.ANY),
+        out_specs=pl.BlockSpec(memory_space=pltpu.VMEM),
         scratch_shapes=[
             pltpu.VMEM(rows.shape, f32),
             pltpu.VMEM((2, 2, levels, layers, cells, SUB, LANES), f32),
@@ -524,7 +507,6 @@
             pltpu.VMEM((6 * levels + 6, every, LANES), f32),
             pltpu.VMEM((6 * levels + 6, 2 * cells, LANES), f32),
             dma((3,)),
-            dma((3,)),
             dma((STEPS, 2)),
             dma((STEPS, 2)),
             dma((STEPS, 2)),

time: 45.2 us -> 42.7 us (0.945)
  Pallas kernels: 42.1 us -> 39.2 us
    pallas_call x1, Pallas kernels: 42.1 us -> 39.2 us  [local(): pl.pallas_call(functools.partial(kernel, layers, cells, levels, spaces, v...]
where the time goes in v2:
time: 42.7 us; the launch traced here: 42.2 us
  Pallas kernels  39.2 us (92%)
  local copies, waits for them, and re-layouts  2.99 us (7%)
    pallas_call x1, Pallas kernels, local(): pl.pallas_call(functools.partial(kernel, layers, cells, levels, spaces, v...  39.2 us
    unnamed x3, local copies, waits for them, and re-layouts  2.99 us

profile of v2, /device:TPU:8, one launch (start us, length us, event | category | flops | bytes accessed | tf_op | source)
XLA Modules:
  0.0 42.2 jit_solution(16606520670916562397)
XLA Ops:
  0.0 0.0 copy-start
  0.0 1.0 %copy-done = bf16[1280,128]{1,0:T(8,128)(2,1)S(1)} copy-done((bf16[1280,128]{1,0:T(8,128)(2,1)S(1)}, bf16[1280,128]{1,0:T(8,128)(2,1)}, u32[]{:S(2)}) %copy-start) | copy-done | bytes 327704
  1.0 39.2 %shard_map.28 = f32[128,64,128]{2,1,0:T(8,128)S(1)} custom-call(f32[128,64,128]{2,1,0:T(8,128)} %bitcast.11, bf16[1280,128]{1,0:T(8,128)(2,1)S(1)} %copy-done), custom_call_target="tpu_custom_call" | custom-call | tf_op jit(solution)/shard_map/pallas_call | solution.py:486
  40.2 2.0 %copy.6 = f32[8,4,4,2,4096]{4,3,2,1,0:T(2,128)} copy(f32[8,4,4,2,4096]{4,3,2,1,0:T(2,128)S(1)} %bitcast.10) | data formatting | bytes 8388608
Async XLA Ops:
  0.0 1.0 %copy-start = (bf16[1280,128]{1,0:T(8,128)(2,1)S(1)}, bf16[1280,128]{1,0:T(8,128)(2,1)}, u32[]{:S(2)}) copy-start(bf16[1280,128]{1,0:T(8,128)(2,1)} %constant.2.clone.w_ref) | copy-start | bytes 983044
